TPU v7x, 32 devices: a whole 2x2x4 slice. The times are simulated.
32 devices in a mesh: seq: 16 (over z, x, core), head: 2 (over y).
Axes of the slice: x: 2, y: 2, z: 4, core: 2. Of those that a mesh axis runs over, the one named last changes fastest.
Arguments:
- queries: bfloat16 [1, 4096, 16, 128], P(None, 'seq', 'head'), may hold values from -6 to 6
- keys: bfloat16 [1, 4096, 4, 128], P(None, 'seq', 'head'), may hold values from -6 to 6
- values: bfloat16 [1, 4096, 4, 128], P(None, 'seq', 'head'), may hold values from -6 to 6
- norm_gain: float32 [16, 128], P('head'), may hold values from 0.25 to 1.75
- out_grad: bfloat16 [1, 4096, 16, 128], P(None, 'seq', 'head'), may hold values from -6 to 6
- window_reach: int32 [1, 16], P(None, 'seq'), may hold values from 0 to 256
- partner_mask: int32 [1, 16, 3], P(None, 'seq'), may hold values 0 or 1
Outputs:
- normed: bfloat16 [1, 4096, 16, 128], P(None, 'seq', 'head')
- query_grad: bfloat16 [1, 4096, 16, 128], P(None, 'seq', 'head')
- key_gradient: bfloat16 [1, 4096, 4, 128], P(None, 'seq', 'head')
- value_gradient: bfloat16 [1, 4096, 4, 128], P(None, 'seq', 'head')
All inputs are finite; a program needn't handle non-finite values. No bound on the sum of `partner_mask` on one device may be relied on, other than what follows from the above.
Results may differ from a plain program's by a relative error of at most 0.029.
Values may be sent and summed in bfloat16 or wider, within the bound.
A program may use at most 64 MiB of HBM per device.

v0:
```python
import math

import jax
import jax.numpy as jnp
from jax import lax
from jax.sharding import PartitionSpec as P

epsilon = 1e-06


def passed_along(value, axis, steps):
    count = lax.axis_size(axis)
    leading, last = (max(0, -steps), min(count, count - steps))
    return lax.ppermute(value, axis, [(source, source + steps) for source in range(leading, last)])


def per_device(queries, keys, values, norm_gain, out_grad, window_reach, partner_mask):
    batch_size, block_rows, local_heads, head_size = queries.shape
    key_heads = keys.shape[2]
    group_size = local_heads // key_heads
    score_scale = 1.0 / math.sqrt(head_size)
    device_count = lax.axis_size("seq")
    my_block = lax.axis_index("seq")
    level_count = len([level for level in range(1, 11) if 2 ** (level + 1) <= device_count])
    grouped = queries.reshape(batch_size, block_rows, key_heads, group_size, head_size)
    window_pair = passed_along((keys, values), "seq", 1)
    partner_pairs = []
    for level in range(1, level_count + 1):
        partner_pairs.append(passed_along((keys, values), "seq", 2**level))
    query_pos = lax.broadcasted_iota(jnp.int32, (block_rows, block_rows), 0)
    key_pos = lax.broadcasted_iota(jnp.int32, (block_rows, block_rows), 1)
    own_mask = (key_pos <= query_pos)[None, None, None]
    window_mask = (
        (key_pos[None] >= block_rows - window_reach[:, 0][:, None, None]) & (my_block >= 1)
    )[:, None, None]
    block_list = [(keys, values, own_mask), (window_pair[0], window_pair[1], window_mask)]
    for level in range(1, level_count + 1):
        level_on = (partner_mask[:, 0, level - 1] == 1) & (my_block >= 2**level)
        block_list.append(
            (
                partner_pairs[level - 1][0],
                partner_pairs[level - 1][1],
                level_on[:, None, None, None, None],
            )
        )

    def scores_of(key_block, key_mask):
        raw_scores = (
            jnp.einsum("buhgd,bshd->bhgus", grouped, key_block, preferred_element_type=jnp.float32)
            * score_scale
        )
        return jnp.where(key_mask, raw_scores, -jnp.inf)

    score_list = [scores_of(key_block, key_mask) for key_block, value_block, key_mask in block_list]
    running = jnp.max(score_list[0], axis=-1)
    exp_total = jnp.sum(jnp.exp(score_list[0] - running[..., None]), axis=-1)
    for current in score_list[1:]:
        updated = jnp.maximum(running, jnp.max(current, axis=-1))
        exp_total = exp_total * jnp.exp(running - updated) + jnp.sum(
            jnp.exp(current - updated[..., None]), axis=-1
        )
        running = updated
    log_total = running + jnp.log(exp_total)
    weight_list = [jnp.exp(current - log_total[..., None]) for current in score_list]
    prob_list = [weights.astype(jnp.bfloat16) for weights in weight_list]
    accumulated = jnp.zeros(grouped.shape, jnp.float32)
    for entry, probabilities in zip(block_list, prob_list):
        accumulated = accumulated + jnp.einsum(
            "bhgus,bshd->buhgd", probabilities, entry[1], preferred_element_type=jnp.float32
        )
    attention = accumulated.astype(jnp.bfloat16).reshape(
        batch_size, block_rows, local_heads, head_size
    )
    features = local_heads * lax.axis_size("head") * head_size
    attn_wide = attention.astype(jnp.float32)
    square_total = lax.psum(jnp.sum(attn_wide * attn_wide, axis=(2, 3)), "head")
    inverse = lax.rsqrt(square_total / features + epsilon)
    normed = (norm_gain * attn_wide * inverse[..., None, None]).astype(jnp.bfloat16)
    scaled_grad = norm_gain * out_grad.astype(jnp.float32)
    dot_total = lax.psum(jnp.sum(scaled_grad * attn_wide, axis=(2, 3)), "head")
    attention_gradient = (
        scaled_grad * inverse[..., None, None]
        - attn_wide * (dot_total * inverse**3 / features)[..., None, None]
    ).astype(jnp.bfloat16)
    correction_rows = jnp.sum(attention_gradient.astype(jnp.float32) * attn_wide, axis=-1)
    correction_rows = correction_rows.reshape(
        batch_size, block_rows, key_heads, group_size
    ).transpose(0, 2, 3, 1)
    grad_grouped = attention_gradient.reshape(
        batch_size, block_rows, key_heads, group_size, head_size
    )
    query_acc = jnp.zeros(grouped.shape, jnp.float32)
    partials = []
    for entry, weights, probabilities in zip(block_list, weight_list, prob_list):
        key_block, value_block = (entry[0], entry[1])
        prob_grad = jnp.einsum(
            "buhgd,bshd->bhgus", grad_grouped, value_block, preferred_element_type=jnp.float32
        )
        score_grad = (weights * (prob_grad - correction_rows[..., None])).astype(jnp.bfloat16)
        query_acc = query_acc + jnp.einsum(
            "bhgus,bshd->buhgd", score_grad, key_block, preferred_element_type=jnp.float32
        )
        key_part = jnp.einsum(
            "bhgus,buhgd->bshd", score_grad, grouped, preferred_element_type=jnp.float32
        )
        value_part = jnp.einsum(
            "bhgus,buhgd->bshd", probabilities, grad_grouped, preferred_element_type=jnp.float32
        )
        partials.append((key_part, value_part))
    key_sum, value_sum = partials[0]
    nearest = partials[1]
    for level in range(1, level_count + 1):
        level_part = partials[level + 1]
        arrived = (
            passed_along(level_part[0].astype(jnp.bfloat16), "seq", -(2**level)).astype(
                jnp.float32
            ),
            passed_along(level_part[1].astype(jnp.bfloat16), "seq", -(2**level)).astype(
                jnp.float32
            ),
        )
        key_sum = key_sum + arrived[0]
        value_sum = value_sum + arrived[1]
    arrived = (
        passed_along(nearest[0].astype(jnp.bfloat16), "seq", -1).astype(jnp.float32),
        passed_along(nearest[1].astype(jnp.bfloat16), "seq", -1).astype(jnp.float32),
    )
    key_sum = key_sum + arrived[0]
    value_sum = value_sum + arrived[1]
    query_grad = (
        (query_acc * score_scale)
        .astype(jnp.bfloat16)
        .reshape(batch_size, block_rows, local_heads, head_size)
    )
    key_gradient = (key_sum * score_scale).astype(jnp.bfloat16)
    value_gradient = value_sum.astype(jnp.bfloat16)
    return (normed, query_grad, key_gradient, value_gradient)


def solution(mesh):
    return jax.shard_map(
        per_device,
        mesh=mesh,
        in_specs=(
            P(None, "seq", "head", None),
            P(None, "seq", "head", None),
            P(None, "seq", "head", None),
            P("head", None),
            P(None, "seq", "head", None),
            P(None, "seq"),
            P(None, "seq", None),
        ),
        out_specs=(
            P(None, "seq", "head", None),
            P(None, "seq", "head", None),
            P(None, "seq", "head", None),
            P(None, "seq", "head", None),
        ),
        check_vma=False,
    )
```

profile of v0, /device:TPU:11, one launch (start us, length us, event | category | flops | bytes accessed | tf_op | source)
XLA Modules:
  0.0 116.8 jit_solution(584869146604829191)
XLA Ops:
  0.6 1.7 %copy.150 = bf16[1,256,2,128]{1,3,2,0:T(8,128)(2,1)} copy(bf16[1,256,2,128]{3,2,1,0:T(2,128)(2,1)} %param.9) | data formatting | bytes 262144 | tf_op args[2]
  2.4 4.2 %collective-permute-start.7 = (bf16[1,256,2,128]{1,3,2,0:T(8,128)(2,1)}, bf16[1,256,2,128]{1,3,2,0:T(8,128)(2,1)S(1)}, u32[]{:S(2)}, u32[]{:S(2)}) collective-permute-start(bf16[1,256,2,128]{1,3,2,0:T(8,128)(2,1)} %copy.150), channel_id=1, source_target_pairs={{0,16},{2,18},{4,20},{6,22},{8,24},{10,26},{12,28},{14,30},{1,17},... | collective-permute-start | bytes 393224 | tf_op jit(solution)/shard_map/ppermute | solution.py:14
  6.6 1.9 %collective-permute-start.6 = (bf16[1,256,2,128]{1,3,2,0:T(8,128)(2,1)}, bf16[1,256,2,128]{1,3,2,0:T(8,128)(2,1)S(1)}, u32[]{:S(2)}, u32[]{:S(2)}) collective-permute-start(bf16[1,256,2,128]{1,3,2,0:T(8,128)(2,1)} %copy.150), channel_id=1, source_target_pairs={{0,8},{2,10},{4,12},{6,14},{8,16},{10,18},{12,20},{14,22},{16,24},... | collective-permute-start | bytes 393224 | tf_op jit(solution)/shard_map/ppermute | solution.py:14
  8.5 1.9 %collective-permute-start.5 = (bf16[1,256,2,128]{1,3,2,0:T(8,128)(2,1)}, bf16[1,256,2,128]{1,3,2,0:T(8,128)(2,1)S(1)}, u32[]{:S(2)}, u32[]{:S(2)}) collective-permute-start(bf16[1,256,2,128]{1,3,2,0:T(8,128)(2,1)} %copy.150), channel_id=1, source_target_pairs={{0,4},{2,6},{4,8},{6,10},{8,12},{10,14},{12,16},{14,18},{16,20},{1... | collective-permute-start | bytes 393224 | tf_op jit(solution)/shard_map/ppermute | solution.py:14
  10.4 3.9 %collective-permute-start.4 = (bf16[1,256,2,128]{1,3,2,0:T(8,128)(2,1)}, bf16[1,256,2,128]{1,3,2,0:T(8,128)(2,1)}, u32[]{:S(2)}, u32[]{:S(2)}) collective-permute-start(bf16[1,256,2,128]{1,3,2,0:T(8,128)(2,1)} %copy.150), channel_id=1, source_target_pairs={{0,2},{2,4},{4,6},{6,8},{8,10},{10,12},{12,14},{14,16},{16,18},{18... | collective-permute-start | bytes 393224 | tf_op jit(solution)/shard_map/ppermute | solution.py:14
  14.3 0.9 copy.140
  15.2 1.9 %collective-permute-start = (bf16[1,256,2,128]{3,1,2,0:T(8,128)(2,1)S(1)}, bf16[1,256,2,128]{3,1,2,0:T(8,128)(2,1)S(1)}, u32[]{:S(2)}, u32[]{:S(2)}) collective-permute-start(bf16[1,256,2,128]{3,1,2,0:T(8,128)(2,1)S(1)} %copy.140), channel_id=1, source_target_pairs={{0,2},{2,4},{4,6},{6,8},{8,10},{10,12},{12,14},{14,16},{16,18},{18... | collective-permute-start | bytes 393224 | tf_op jit(solution)/shard_map/ppermute | solution.py:14
  17.2 1.4 %fusion.109 = (f32[2,4,256]{2,1,0:T(4,128)S(1)}, f32[1,2,4,256,256]{3,4,2,1,0:T(8,128)S(1)}) fusion(bf16[256,2,4,128]{3,2,1,0:T(4,128)(2,1)S(1)} %bitcast.458, bf16[256,2,128,1]{2,1,0,3:T(2,128)(2,1)} %bitcast.486, pred[256,256]{0,1:T(8,128)(4,1)S(1)} %iota_compare_fusion.1), kind=kOutput, calls=%fused_computation.147 | convolution fusion | flops 135788544 | bytes 2826240 | tf_op jit(solution)/shard_map/buhgd,bshd->bhgus/dot_general | solution.py:49
  18.7 0.9 exponential_reduce_fusion.1
  19.6 0.6 fusion.108
  23.0 1.9 %collective-permute-start.1 = (bf16[1,256,2,128]{3,1,2,0:T(8,128)(2,1)}, bf16[1,256,2,128]{3,1,2,0:T(8,128)(2,1)S(1)}, u32[]{:S(2)}, u32[]{:S(2)}) collective-permute-start(bf16[1,256,2,128]{3,1,2,0:T(8,128)(2,1)} %copy-done.24), channel_id=1, source_target_pairs={{0,4},{2,6},{4,8},{6,10},{8,12},{10,14},{12,16},{14,18},{16,20},{1... | collective-permute-start | bytes 393224 | tf_op jit(solution)/shard_map/ppermute | solution.py:14
  25.4 4.2 %collective-permute-done.1 = bf16[1,256,2,128]{3,1,2,0:T(8,128)(2,1)S(1)} collective-permute-done((bf16[1,256,2,128]{3,1,2,0:T(8,128)(2,1)}, bf16[1,256,2,128]{3,1,2,0:T(8,128)(2,1)S(1)}, u32[]{:S(2)}, u32[]{:S(2)}) %collective-permute-start.1) | collective-permute-done | bytes 131104 | tf_op jit(solution)/shard_map/ppermute | solution.py:14
  29.7 1.9 %collective-permute-start.2 = (bf16[1,256,2,128]{3,1,2,0:T(8,128)(2,1)S(1)}, bf16[1,256,2,128]{3,1,2,0:T(8,128)(2,1)S(1)}, u32[]{:S(2)}, u32[]{:S(2)}) collective-permute-start(bf16[1,256,2,128]{3,1,2,0:T(8,128)(2,1)S(1)} %copy-done.25), channel_id=1, source_target_pairs={{0,8},{2,10},{4,12},{6,14},{8,16},{10,18},{12,20},{14,22},{16,24},... | collective-permute-start | bytes 393224 | tf_op jit(solution)/shard_map/ppermute | solution.py:14
  32.1 3.3 %collective-permute-done.2 = bf16[1,256,2,128]{3,1,2,0:T(8,128)(2,1)S(1)} collective-permute-done((bf16[1,256,2,128]{3,1,2,0:T(8,128)(2,1)S(1)}, bf16[1,256,2,128]{3,1,2,0:T(8,128)(2,1)S(1)}, u32[]{:S(2)}, u32[]{:S(2)}) %collective-permute-start.2) | collective-permute-done | bytes 131104 | tf_op jit(solution)/shard_map/ppermute | solution.py:14
  35.4 1.3 %collective-permute-start.3 = (bf16[1,256,2,128]{3,1,2,0:T(8,128)(2,1)S(1)}, bf16[1,256,2,128]{3,1,2,0:T(8,128)(2,1)S(1)}, u32[]{:S(2)}, u32[]{:S(2)}) collective-permute-start(bf16[1,256,2,128]{3,1,2,0:T(8,128)(2,1)S(1)} %copy-done.25), channel_id=1, source_target_pairs={{0,16},{2,18},{4,20},{6,22},{8,24},{10,26},{12,28},{14,30},{1,17},... | collective-permute-start | bytes 393224 | tf_op jit(solution)/shard_map/ppermute | solution.py:14
  37.1 1.4 %collective-permute-done.3 = bf16[1,256,2,128]{3,1,2,0:T(8,128)(2,1)S(1)} collective-permute-done((bf16[1,256,2,128]{3,1,2,0:T(8,128)(2,1)S(1)}, bf16[1,256,2,128]{3,1,2,0:T(8,128)(2,1)S(1)}, u32[]{:S(2)}, u32[]{:S(2)}) %collective-permute-start.3) | collective-permute-done | bytes 131104 | tf_op jit(solution)/shard_map/ppermute | solution.py:14
  39.3 0.6 fusion.17
  39.9 0.6 fusion.11
  40.6 0.5 fusion.59
  41.1 1.4 %convolution_add_fusion.1 = f32[2,4,256,128]{2,3,1,0:T(8,128)S(1)} fusion(f32[2,4,256,128]{2,3,1,0:T(8,128)S(1)} %fusion.59, f32[1,2,4,256,256]{3,4,2,1,0:T(8,128)S(1)} %get-tuple-element.39, f32[2,4,256]{2,1,0:T(4,128)S(1)} %bitcast.470, bf16[1,256,2,128]{1,3,2,0:T(8,128)(2,1)} %collective-permute-done.4), kind=kOutput, calls=%fused_computation.54 | convolution fusion | flops 135528448 | bytes 4333568 | tf_op jit(solution)/shard_map/bhgus,bshd->buhgd/dot_general | solution.py:68
  42.6 0.5 fusion.66
  43.1 0.5 fusion.69
  43.7 0.7 copy-done.22
  44.4 2.2 %multiply_reduce_fusion = (f32[256]{0:T(256)}, f32[2,4,256,128]{2,3,1,0:T(8,128)}) fusion(f32[2,4,256,128]{2,3,1,0:T(8,128)S(1)} %fusion.69, f32[2,4,256,128]{2,3,1,0:T(8,128)S(1)} %fusion.66, f32[2,4,256,128]{2,3,1,0:T(8,128)S(1)} %convolution_add_fusion.1, f32[2,256,256,4]{2,1,3,0:T(8,128)S(1)} %get-tuple-element.35, f32[2,4,256]{2,1,0:T(4,128)S(1)} %bitcast.473, ...), kind=kOutput, calls=%fused_computation.95 | convolution fusion | flops 137101056 | bytes 6431744 | tf_op jit(solution)/shard_map/bhgus,bshd->buhgd/dot_general | solution.py:68
  46.6 2.6 %copy.158 = f32[1,256,8,128]{3,2,1,0:T(8,128)} copy(f32[1,256,8,128]{1,3,2,0:T(8,128)} %bitcast.468) | data formatting | bytes 2097152 | tf_op jit(solution)/shard_map/convert_element_type | solution.py:75
  49.2 2.3 %multiply_reduce_fusion.2 = f32[256]{0:T(256)S(1)} fusion(f32[1,256,8,128]{3,2,1,0:T(8,128)} %copy.158, bf16[1,256,8,128]{3,2,1,0:T(8,128)(2,1)S(1)} %copy-done.11, f32[8,128]{1,0:T(8,128)S(1)} %copy-done.30), kind=kLoop, calls=%fused_computation.98 | loop fusion | flops 1048320 | bytes 1577984 | tf_op jit(solution)/shard_map/reduce_sum | solution.py:80
  51.4 4.7 %all-reduce = (f32[1,256]{1,0:T(1,128)}, f32[1,256]{1,0:T(1,128)}) all-reduce(f32[1,256]{1,0:T(1,128)} %bitcast.512, f32[1,256]{1,0:T(1,128)S(1)} %bitcast.511), channel_id=1, replica_groups=mesh['seq'=16,'head'=2] {'head'}, use_global_device_ids=true, to_apply=%region_11.12 | all-reduce | flops 512 | bytes 4096 | tf_op jit(solution)/shard_map/psum | solution.py:76
  56.1 0.7 fusion.94
  56.8 4.0 %multiply_reduce_fusion.1 = (f32[256,8]{1,0:T(8,128)}, bf16[1,256,8,128]{3,2,1,0:T(8,128)(2,1)}, bf16[1,256,8,128]{3,2,1,0:T(8,128)(2,1)}) fusion(f32[1,256,8,128]{3,2,1,0:T(8,128)} %copy.158, f32[256]{0:T(256)S(1)} %bitcast.509, f32[256]{0:T(256)S(1)} %bitcast.510, bf16[1,256,8,128]{3,2,1,0:T(8,128)(2,1)S(1)} %copy-done.11, f32[8,128]{1,0:T(8,128)S(1)} %copy-done.30), kind=kLoop, calls=%fused_computation.96 | loop fusion | flops 3143680 | bytes 2635776 | tf_op jit(solution)/shard_map/reduce_sum | solution.py:85
  60.9 1.3 %copy.189 = bf16[256,2,4,128]{0,3,2,1:T(8,128)(2,1)S(1)} copy(bf16[256,2,4,128]{3,2,1,0:T(4,128)(2,1)} %bitcast.485) | data formatting | bytes 1048576 | tf_op jit(solution)/shard_map/reshape.58
  62.2 2.9 %fusion.45 = bf16[1,256,2,128]{1,3,2,0:T(8,128)(2,1)} fusion(bf16[256,2,4,128]{0,3,2,1:T(8,128)(2,1)S(1)} %copy.189, f32[1,2,4,256,256]{3,4,2,1,0:T(8,128)} %copy-done.3, f32[2,4,256]{2,1,0:T(4,128)S(1)} %bitcast.474), kind=kOutput, calls=%fused_computation.82 | convolution fusion | flops 135331840 | bytes 2760704 | tf_op jit(solution)/shard_map/bhgus,buhgd->bshd/dot_general | solution.py:106
  65.1 1.2 fusion.46
  66.3 1.2 %fusion.48 = bf16[1,256,2,128]{1,3,2,0:T(8,128)(2,1)} fusion(bf16[256,2,4,128]{0,3,2,1:T(8,128)(2,1)S(1)} %copy.189, f32[2,256,256,4]{2,1,3,0:T(8,128)S(1)} %copy-done.9, f32[2,4,256]{2,1,0:T(4,128)S(1)} %bitcast.476), kind=kOutput, calls=%fused_computation.85 | convolution fusion | flops 135331840 | bytes 2760704 | tf_op jit(solution)/shard_map/bhgus,buhgd->bshd/dot_general | solution.py:106
  67.4 1.6 %copy.165 = f32[256,8]{0,1:T(8,128)} copy(f32[256,8]{1,0:T(8,128)} %get-tuple-element.18) | data formatting | bytes 16384 | tf_op jit(solution)/shard_map/reduce_sum | solution.py:85
  69.0 0.7 reshape.467
  69.7 0.6 fusion.24
  70.3 1.0 copy-done.4
  71.3 1.7 %fusion.25 = bf16[2,4,256,256]{2,3,1,0:T(8,128)(2,1)S(1)} fusion(bf16[256,2,4,128]{0,3,2,1:T(8,128)(2,1)S(1)} %copy.189, f32[1,2,4,256,256]{3,4,2,1,0:T(8,128)S(1)} %copy-done.4, f32[2,4,256]{2,1,0:T(4,128)S(1)} %bitcast.490, f32[2,4,256]{2,1,0:T(4,128)S(1)} %bitcast.478, bf16[1,256,2,128]{1,3,2,0:T(8,128)(2,1)} %collective-permute-done.4), kind=kOutput, calls=%fused_computation.48 | convolution fusion | flops 136314880 | bytes 3817472 | tf_op jit(solution)/shard_map/buhgd,bshd->bhgus/dot_general | solution.py:96
  73.4 0.6 fusion.28
  74.5 0.5 copy-done.2
  75.0 0.6 fusion.27
  76.1 0.5 copy-done.10
  76.6 0.6 fusion.26
  77.7 3.9 %collective-permute-start.8 = (bf16[1,256,2,128]{3,1,2,0:T(8,128)(2,1)S(1)}, bf16[1,256,2,128]{3,1,2,0:T(8,128)(2,1)S(1)}, u32[]{:S(2)}, u32[]{:S(2)}) collective-permute-start(bf16[1,256,2,128]{3,1,2,0:T(8,128)(2,1)S(1)} %fusion.52), channel_id=1, source_target_pairs={{4,0},{6,2},{8,4},{10,6},{12,8},{14,10},{16,12},{18,14},{20,16},{2... | collective-permute-start | bytes 393224 | tf_op jit(solution)/shard_map/ppermute | solution.py:14
  81.6 3.0 %collective-permute-start.12 = (bf16[1,256,2,128]{1,3,2,0:T(8,128)(2,1)S(1)}, bf16[1,256,2,128]{1,3,2,0:T(8,128)(2,1)S(1)}, u32[]{:S(2)}, u32[]{:S(2)}) collective-permute-start(bf16[1,256,2,128]{1,3,2,0:T(8,128)(2,1)S(1)} %copy-done.28), channel_id=1, source_target_pairs={{4,0},{6,2},{8,4},{10,6},{12,8},{14,10},{16,12},{18,14},{20,16},{2... | collective-permute-start | bytes 393224 | tf_op jit(solution)/shard_map/ppermute | solution.py:14
  84.6 2.6 %collective-permute-start.9 = (bf16[1,256,2,128]{3,1,2,0:T(8,128)(2,1)S(1)}, bf16[1,256,2,128]{3,1,2,0:T(8,128)(2,1)S(1)}, u32[]{:S(2)}, u32[]{:S(2)}) collective-permute-start(bf16[1,256,2,128]{3,1,2,0:T(8,128)(2,1)S(1)} %fusion.51), channel_id=1, source_target_pairs={{8,0},{10,2},{12,4},{14,6},{16,8},{18,10},{20,12},{22,14},{24,16},... | collective-permute-start | bytes 393224 | tf_op jit(solution)/shard_map/ppermute | solution.py:14
  87.2 1.3 %collective-permute-start.10 = (bf16[1,256,2,128]{3,1,2,0:T(8,128)(2,1)S(1)}, bf16[1,256,2,128]{3,1,2,0:T(8,128)(2,1)S(1)}, u32[]{:S(2)}, u32[]{:S(2)}) collective-permute-start(bf16[1,256,2,128]{3,1,2,0:T(8,128)(2,1)S(1)} %fusion.50), channel_id=1, source_target_pairs={{16,0},{18,2},{20,4},{22,6},{24,8},{26,10},{28,12},{30,14},{17,1},... | collective-permute-start | bytes 393224 | tf_op jit(solution)/shard_map/ppermute | solution.py:14
  88.5 7.1 %collective-permute-start.11 = (bf16[1,256,2,128]{3,1,2,0:T(8,128)(2,1)S(1)}, bf16[1,256,2,128]{3,1,2,0:T(8,128)(2,1)S(1)}, u32[]{:S(2)}, u32[]{:S(2)}) collective-permute-start(bf16[1,256,2,128]{3,1,2,0:T(8,128)(2,1)S(1)} %fusion.49), channel_id=1, source_target_pairs={{2,0},{4,2},{6,4},{8,6},{10,8},{12,10},{14,12},{16,14},{18,16},{20... | collective-permute-start | bytes 393224 | tf_op jit(solution)/shard_map/ppermute | solution.py:14
  95.7 0.5 fusion.90
  96.2 0.6 fusion.80
  96.8 0.6 fusion.83
  97.3 0.6 convolution_add_fusion.3
  97.9 0.6 fusion.35
  98.5 1.1 copy.199
  99.7 0.5 fusion.47
  100.2 1.9 %collective-permute-start.13 = (bf16[1,256,2,128]{1,3,2,0:T(8,128)(2,1)S(1)}, bf16[1,256,2,128]{1,3,2,0:T(8,128)(2,1)S(1)}, u32[]{:S(2)}, u32[]{:S(2)}) collective-permute-start(bf16[1,256,2,128]{1,3,2,0:T(8,128)(2,1)S(1)} %fusion.47), channel_id=1, source_target_pairs={{8,0},{10,2},{12,4},{14,6},{16,8},{18,10},{20,12},{22,14},{24,16},... | collective-permute-start | bytes 393224 | tf_op jit(solution)/shard_map/ppermute | solution.py:14
  102.1 1.3 %collective-permute-start.14 = (bf16[1,256,2,128]{1,3,2,0:T(8,128)(2,1)S(1)}, bf16[1,256,2,128]{1,3,2,0:T(8,128)(2,1)S(1)}, u32[]{:S(2)}, u32[]{:S(2)}) collective-permute-start(bf16[1,256,2,128]{1,3,2,0:T(8,128)(2,1)S(1)} %copy-done.27), channel_id=1, source_target_pairs={{16,0},{18,2},{20,4},{22,6},{24,8},{26,10},{28,12},{30,14},{17,1},... | collective-permute-start | bytes 393224 | tf_op jit(solution)/shard_map/ppermute | solution.py:14
  103.5 1.9 %collective-permute-start.15 = (bf16[1,256,2,128]{1,3,2,0:T(8,128)(2,1)S(1)}, bf16[1,256,2,128]{1,3,2,0:T(8,128)(2,1)S(1)}, u32[]{:S(2)}, u32[]{:S(2)}) collective-permute-start(bf16[1,256,2,128]{1,3,2,0:T(8,128)(2,1)S(1)} %copy-done.26), channel_id=1, source_target_pairs={{2,0},{4,2},{6,4},{8,6},{10,8},{12,10},{14,12},{16,14},{18,16},{20... | collective-permute-start | bytes 393224 | tf_op jit(solution)/shard_map/ppermute | solution.py:14
  105.8 0.8 copy.200
  106.6 0.8 collective-permute-done.13
  107.4 3.9 %collective-permute-done.14 = bf16[1,256,2,128]{1,3,2,0:T(8,128)(2,1)S(1)} collective-permute-done((bf16[1,256,2,128]{1,3,2,0:T(8,128)(2,1)S(1)}, bf16[1,256,2,128]{1,3,2,0:T(8,128)(2,1)S(1)}, u32[]{:S(2)}, u32[]{:S(2)}) %collective-permute-start.14) | collective-permute-done | bytes 131104 | tf_op jit(solution)/shard_map/ppermute | solution.py:14
  111.4 4.1 %collective-permute-done.15 = bf16[1,256,2,128]{1,3,2,0:T(8,128)(2,1)S(1)} collective-permute-done((bf16[1,256,2,128]{1,3,2,0:T(8,128)(2,1)S(1)}, bf16[1,256,2,128]{1,3,2,0:T(8,128)(2,1)S(1)}, u32[]{:S(2)}, u32[]{:S(2)}) %collective-permute-start.15) | collective-permute-done | bytes 131104 | tf_op jit(solution)/shard_map/ppermute | solution.py:14
  115.5 0.5 add_convert_fusion
  116.1 0.8 copy.201
  (84 shorter events, 4.7 us)
Async XLA Ops:
  0.6 16.6 %copy-start = (bf16[1,256,8,128]{3,2,1,0:T(8,128)(2,1)S(1)}, bf16[1,256,8,128]{3,2,1,0:T(8,128)(2,1)}, u32[]{:S(2)}) copy-start(bf16[1,256,8,128]{3,2,1,0:T(8,128)(2,1)} %param.7) | copy-start | bytes 1572868
  2.4 40.7 %collective-permute-start.7 = (bf16[1,256,2,128]{1,3,2,0:T(8,128)(2,1)}, bf16[1,256,2,128]{1,3,2,0:T(8,128)(2,1)S(1)}, u32[]{:S(2)}, u32[]{:S(2)}) collective-permute-start(bf16[1,256,2,128]{1,3,2,0:T(8,128)(2,1)} %copy.150), channel_id=1, source_target_pairs={{0,16},{2,18},{4,20},{6,22},{8,24},{10,26},{12,28},{14,30},{1,17},... | collective-permute-start | bytes 393224 | tf_op jit(solution)/shard_map/ppermute | solution.py:14
  6.6 35.9 %collective-permute-start.6 = (bf16[1,256,2,128]{1,3,2,0:T(8,128)(2,1)}, bf16[1,256,2,128]{1,3,2,0:T(8,128)(2,1)S(1)}, u32[]{:S(2)}, u32[]{:S(2)}) collective-permute-start(bf16[1,256,2,128]{1,3,2,0:T(8,128)(2,1)} %copy.150), channel_id=1, source_target_pairs={{0,8},{2,10},{4,12},{6,14},{8,16},{10,18},{12,20},{14,22},{16,24},... | collective-permute-start | bytes 393224 | tf_op jit(solution)/shard_map/ppermute | solution.py:14
  8.5 35.1 %collective-permute-start.5 = (bf16[1,256,2,128]{1,3,2,0:T(8,128)(2,1)}, bf16[1,256,2,128]{1,3,2,0:T(8,128)(2,1)S(1)}, u32[]{:S(2)}, u32[]{:S(2)}) collective-permute-start(bf16[1,256,2,128]{1,3,2,0:T(8,128)(2,1)} %copy.150), channel_id=1, source_target_pairs={{0,4},{2,6},{4,8},{6,10},{8,12},{10,14},{12,16},{14,18},{16,20},{1... | collective-permute-start | bytes 393224 | tf_op jit(solution)/shard_map/ppermute | solution.py:14
  10.4 30.6 %collective-permute-start.4 = (bf16[1,256,2,128]{1,3,2,0:T(8,128)(2,1)}, bf16[1,256,2,128]{1,3,2,0:T(8,128)(2,1)}, u32[]{:S(2)}, u32[]{:S(2)}) collective-permute-start(bf16[1,256,2,128]{1,3,2,0:T(8,128)(2,1)} %copy.150), channel_id=1, source_target_pairs={{0,2},{2,4},{4,6},{6,8},{8,10},{10,12},{12,14},{14,16},{16,18},{18... | collective-permute-start | bytes 393224 | tf_op jit(solution)/shard_map/ppermute | solution.py:14
  15.2 4.4 %copy-start.24 = (bf16[1,256,2,128]{3,1,2,0:T(8,128)(2,1)}, bf16[1,256,2,128]{3,1,2,0:T(8,128)(2,1)S(1)}, u32[]{:S(2)}) copy-start(bf16[1,256,2,128]{3,1,2,0:T(8,128)(2,1)S(1)} %copy.140) | copy-start | bytes 393220
  15.2 7.7 %collective-permute-start = (bf16[1,256,2,128]{3,1,2,0:T(8,128)(2,1)S(1)}, bf16[1,256,2,128]{3,1,2,0:T(8,128)(2,1)S(1)}, u32[]{:S(2)}, u32[]{:S(2)}) collective-permute-start(bf16[1,256,2,128]{3,1,2,0:T(8,128)(2,1)S(1)} %copy.140), channel_id=1, source_target_pairs={{0,2},{2,4},{4,6},{6,8},{8,10},{10,12},{12,14},{14,16},{16,18},{18... | collective-permute-start | bytes 393224 | tf_op jit(solution)/shard_map/ppermute | solution.py:14
  17.2 2.4 %copy-start.31 = (s32[1,1,3]{2,1,0:T(1,128)S(1)}, s32[1,1,3]{2,1,0:T(1,128)}, u32[]{:S(2)}) copy-start(s32[1,1,3]{2,1,0:T(1,128)} %param.13) | copy-start | bytes 40
  17.2 5.6 %copy-start.17 = (bf16[1,256,2,128]{3,2,1,0:T(2,128)(2,1)S(1)}, bf16[1,256,2,128]{3,2,1,0:T(2,128)(2,1)}, u32[]{:S(2)}) copy-start(bf16[1,256,2,128]{3,2,1,0:T(2,128)(2,1)} %param.9) | copy-start | bytes 393220
  22.9 6.7 %copy-start.25 = (bf16[1,256,2,128]{3,1,2,0:T(8,128)(2,1)S(1)}, bf16[1,256,2,128]{3,1,2,0:T(8,128)(2,1)}, u32[]{:S(2)}) copy-start(bf16[1,256,2,128]{3,1,2,0:T(8,128)(2,1)} %copy-done.24) | copy-start | bytes 393220
  23.0 6.7 %collective-permute-start.1 = (bf16[1,256,2,128]{3,1,2,0:T(8,128)(2,1)}, bf16[1,256,2,128]{3,1,2,0:T(8,128)(2,1)S(1)}, u32[]{:S(2)}, u32[]{:S(2)}) collective-permute-start(bf16[1,256,2,128]{3,1,2,0:T(8,128)(2,1)} %copy-done.24), channel_id=1, source_target_pairs={{0,4},{2,6},{4,8},{6,10},{8,12},{10,14},{12,16},{14,18},{16,20},{1... | collective-permute-start | bytes 393224 | tf_op jit(solution)/shard_map/ppermute | solution.py:14
  25.4 15.7 %copy-start.3 = (f32[1,2,4,256,256]{3,4,2,1,0:T(8,128)}, f32[1,2,4,256,256]{3,4,2,1,0:T(8,128)S(1)}, u32[]{:S(2)}) copy-start(f32[1,2,4,256,256]{3,4,2,1,0:T(8,128)S(1)} %get-tuple-element.39) | copy-start | bytes 6291460
  29.7 5.7 %collective-permute-start.2 = (bf16[1,256,2,128]{3,1,2,0:T(8,128)(2,1)S(1)}, bf16[1,256,2,128]{3,1,2,0:T(8,128)(2,1)S(1)}, u32[]{:S(2)}, u32[]{:S(2)}) collective-permute-start(bf16[1,256,2,128]{3,1,2,0:T(8,128)(2,1)S(1)} %copy-done.25), channel_id=1, source_target_pairs={{0,8},{2,10},{4,12},{6,14},{8,16},{10,18},{12,20},{14,22},{16,24},... | collective-permute-start | bytes 393224 | tf_op jit(solution)/shard_map/ppermute | solution.py:14
  32.1 11.6 %copy-start.8 = (f32[2,256,256,4]{2,1,3,0:T(8,128)}, f32[2,256,256,4]{2,1,3,0:T(8,128)S(1)}, u32[]{:S(2)}) copy-start(f32[2,256,256,4]{2,1,3,0:T(8,128)S(1)} %get-tuple-element.35) | copy-start | bytes 6291460
  35.4 3.7 %copy-start.13 = (bf16[1,256,2,128]{3,1,2,0:T(8,128)(2,1)}, bf16[1,256,2,128]{3,1,2,0:T(8,128)(2,1)S(1)}, u32[]{:S(2)}) copy-start(bf16[1,256,2,128]{3,1,2,0:T(8,128)(2,1)S(1)} %collective-permute-done.2) | copy-start | bytes 393220
  35.4 3.2 %collective-permute-start.3 = (bf16[1,256,2,128]{3,1,2,0:T(8,128)(2,1)S(1)}, bf16[1,256,2,128]{3,1,2,0:T(8,128)(2,1)S(1)}, u32[]{:S(2)}, u32[]{:S(2)}) collective-permute-start(bf16[1,256,2,128]{3,1,2,0:T(8,128)(2,1)S(1)} %copy-done.25), channel_id=1, source_target_pairs={{0,16},{2,18},{4,20},{6,22},{8,24},{10,26},{12,28},{14,30},{1,17},... | collective-permute-start | bytes 393224 | tf_op jit(solution)/shard_map/ppermute | solution.py:14
  37.1 5.4 %copy-start.1 = (f32[2,256,256,4]{2,1,3,0:T(8,128)}, f32[2,256,256,4]{2,1,3,0:T(8,128)S(1)}, u32[]{:S(2)}) copy-start(f32[2,256,256,4]{2,1,3,0:T(8,128)S(1)} %get-tuple-element.33) | copy-start | bytes 6291460
  38.6 0.7 copy-start.15
  39.1 4.0 %copy-start.5 = (f32[2,256,256,4]{2,1,3,0:T(8,128)}, f32[2,256,256,4]{2,1,3,0:T(8,128)S(1)}, u32[]{:S(2)}) copy-start(f32[2,256,256,4]{2,1,3,0:T(8,128)S(1)} %get-tuple-element.31) | copy-start | bytes 6291460
  39.9 0.7 copy-start.29
  42.6 1.1 copy-start.20
  43.1 0.6 copy-start.18
  43.7 0.7 copy-start.22
  46.6 2.6 %copy-start.11 = (bf16[1,256,8,128]{3,2,1,0:T(8,128)(2,1)S(1)}, bf16[1,256,8,128]{3,2,1,0:T(8,128)(2,1)}, u32[]{:S(2)}) copy-start(bf16[1,256,8,128]{3,2,1,0:T(8,128)(2,1)} %param.11) | copy-start | bytes 1572868
  46.6 2.6 %copy-start.30 = (f32[8,128]{1,0:T(8,128)S(1)}, f32[8,128]{1,0:T(8,128)}, u32[]{:S(2)}) copy-start(f32[8,128]{1,0:T(8,128)} %param.10) | copy-start | bytes 12292
  62.2 2.9 %copy-start.6 = (f32[2,256,256,4]{2,1,3,0:T(8,128)S(1)}, f32[2,256,256,4]{2,1,3,0:T(8,128)}, u32[]{:S(2)}) copy-start(f32[2,256,256,4]{2,1,3,0:T(8,128)} %copy-done.5) | copy-start | bytes 6291460
  62.2 4.1 %copy-start.9 = (f32[2,256,256,4]{2,1,3,0:T(8,128)S(1)}, f32[2,256,256,4]{2,1,3,0:T(8,128)}, u32[]{:S(2)}) copy-start(f32[2,256,256,4]{2,1,3,0:T(8,128)} %copy-done.8) | copy-start | bytes 6291460
  69.7 1.6 %copy-start.4 = (f32[1,2,4,256,256]{3,4,2,1,0:T(8,128)S(1)}, f32[1,2,4,256,256]{3,4,2,1,0:T(8,128)}, u32[]{:S(2)}) copy-start(f32[1,2,4,256,256]{3,4,2,1,0:T(8,128)} %copy-done.3) | copy-start | bytes 6291460
  71.3 2.1 %copy-start.7 = (f32[2,256,256,4]{2,1,3,0:T(8,128)S(1)}, f32[2,256,256,4]{2,1,3,0:T(8,128)}, u32[]{:S(2)}) copy-start(f32[2,256,256,4]{2,1,3,0:T(8,128)} %copy-done.5) | copy-start | bytes 6291460
  71.3 2.1 %copy-start.19 = (bf16[1,256,2,128]{1,3,2,0:T(8,128)(2,1)S(1)}, bf16[1,256,2,128]{1,3,2,0:T(8,128)(2,1)}, u32[]{:S(2)}) copy-start(bf16[1,256,2,128]{1,3,2,0:T(8,128)(2,1)} %copy-done.18) | copy-start | bytes 393220
  73.4 1.6 %copy-start.2 = (f32[2,256,256,4]{2,1,3,0:T(8,128)S(1)}, f32[2,256,256,4]{2,1,3,0:T(8,128)}, u32[]{:S(2)}) copy-start(f32[2,256,256,4]{2,1,3,0:T(8,128)} %copy-done.1) | copy-start | bytes 6291460
  73.4 1.6 %copy-start.21 = (bf16[1,256,2,128]{1,3,2,0:T(8,128)(2,1)S(1)}, bf16[1,256,2,128]{1,3,2,0:T(8,128)(2,1)}, u32[]{:S(2)}) copy-start(bf16[1,256,2,128]{1,3,2,0:T(8,128)(2,1)} %copy-done.20) | copy-start | bytes 393220
  75.0 1.6 %copy-start.10 = (f32[2,256,256,4]{2,1,3,0:T(8,128)S(1)}, f32[2,256,256,4]{2,1,3,0:T(8,128)}, u32[]{:S(2)}) copy-start(f32[2,256,256,4]{2,1,3,0:T(8,128)} %copy-done.8) | copy-start | bytes 6291460
  75.0 1.6 %copy-start.23 = (bf16[1,256,2,128]{1,3,2,0:T(8,128)(2,1)S(1)}, bf16[1,256,2,128]{1,3,2,0:T(8,128)(2,1)}, u32[]{:S(2)}) copy-start(bf16[1,256,2,128]{1,3,2,0:T(8,128)(2,1)} %copy-done.22) | copy-start | bytes 393220
  76.6 5.0 %copy-start.28 = (bf16[1,256,2,128]{1,3,2,0:T(8,128)(2,1)S(1)}, bf16[1,256,2,128]{1,3,2,0:T(8,128)(2,1)}, u32[]{:S(2)}) copy-start(bf16[1,256,2,128]{1,3,2,0:T(8,128)(2,1)} %fusion.48) | copy-start | bytes 393220
  76.6 19.0 %copy-start.12 = (bf16[1,256,2,128]{3,2,1,0:T(2,128)(2,1)S(1)}, bf16[1,256,2,128]{3,2,1,0:T(2,128)(2,1)}, u32[]{:S(2)}) copy-start(bf16[1,256,2,128]{3,2,1,0:T(2,128)(2,1)} %param.8) | copy-start | bytes 393220
  77.2 19.0 %copy-start.16 = (bf16[1,256,2,128]{3,1,2,0:T(8,128)(2,1)S(1)}, bf16[1,256,2,128]{3,1,2,0:T(8,128)(2,1)}, u32[]{:S(2)}) copy-start(bf16[1,256,2,128]{3,1,2,0:T(8,128)(2,1)} %copy-done.15) | copy-start | bytes 393220
  77.7 19.1 %copy-start.14 = (bf16[1,256,2,128]{3,1,2,0:T(8,128)(2,1)S(1)}, bf16[1,256,2,128]{3,1,2,0:T(8,128)(2,1)}, u32[]{:S(2)}) copy-start(bf16[1,256,2,128]{3,1,2,0:T(8,128)(2,1)} %copy-done.13) | copy-start | bytes 393220
  77.7 22.5 %collective-permute-start.8 = (bf16[1,256,2,128]{3,1,2,0:T(8,128)(2,1)S(1)}, bf16[1,256,2,128]{3,1,2,0:T(8,128)(2,1)S(1)}, u32[]{:S(2)}, u32[]{:S(2)}) collective-permute-start(bf16[1,256,2,128]{3,1,2,0:T(8,128)(2,1)S(1)} %fusion.52), channel_id=1, source_target_pairs={{4,0},{6,2},{8,4},{10,6},{12,8},{14,10},{16,12},{18,14},{20,16},{2... | collective-permute-start | bytes 393224 | tf_op jit(solution)/shard_map/ppermute | solution.py:14
  81.6 25.0 %collective-permute-start.12 = (bf16[1,256,2,128]{1,3,2,0:T(8,128)(2,1)S(1)}, bf16[1,256,2,128]{1,3,2,0:T(8,128)(2,1)S(1)}, u32[]{:S(2)}, u32[]{:S(2)}) collective-permute-start(bf16[1,256,2,128]{1,3,2,0:T(8,128)(2,1)S(1)} %copy-done.28), channel_id=1, source_target_pairs={{4,0},{6,2},{8,4},{10,6},{12,8},{14,10},{16,12},{18,14},{20,16},{2... | collective-permute-start | bytes 393224 | tf_op jit(solution)/shard_map/ppermute | solution.py:14
  84.6 17.5 %collective-permute-start.9 = (bf16[1,256,2,128]{3,1,2,0:T(8,128)(2,1)S(1)}, bf16[1,256,2,128]{3,1,2,0:T(8,128)(2,1)S(1)}, u32[]{:S(2)}, u32[]{:S(2)}) collective-permute-start(bf16[1,256,2,128]{3,1,2,0:T(8,128)(2,1)S(1)} %fusion.51), channel_id=1, source_target_pairs={{8,0},{10,2},{12,4},{14,6},{16,8},{18,10},{20,12},{22,14},{24,16},... | collective-permute-start | bytes 393224 | tf_op jit(solution)/shard_map/ppermute | solution.py:14
  87.2 16.2 %collective-permute-start.10 = (bf16[1,256,2,128]{3,1,2,0:T(8,128)(2,1)S(1)}, bf16[1,256,2,128]{3,1,2,0:T(8,128)(2,1)S(1)}, u32[]{:S(2)}, u32[]{:S(2)}) collective-permute-start(bf16[1,256,2,128]{3,1,2,0:T(8,128)(2,1)S(1)} %fusion.50), channel_id=1, source_target_pairs={{16,0},{18,2},{20,4},{22,6},{24,8},{26,10},{28,12},{30,14},{17,1},... | collective-permute-start | bytes 393224 | tf_op jit(solution)/shard_map/ppermute | solution.py:14
  88.5 16.8 %collective-permute-start.11 = (bf16[1,256,2,128]{3,1,2,0:T(8,128)(2,1)S(1)}, bf16[1,256,2,128]{3,1,2,0:T(8,128)(2,1)S(1)}, u32[]{:S(2)}, u32[]{:S(2)}) collective-permute-start(bf16[1,256,2,128]{3,1,2,0:T(8,128)(2,1)S(1)} %fusion.49), channel_id=1, source_target_pairs={{2,0},{4,2},{6,4},{8,6},{10,8},{12,10},{14,12},{16,14},{18,16},{20... | collective-permute-start | bytes 393224 | tf_op jit(solution)/shard_map/ppermute | solution.py:14
  98.5 3.6 %copy-start.27 = (bf16[1,256,2,128]{1,3,2,0:T(8,128)(2,1)S(1)}, bf16[1,256,2,128]{1,3,2,0:T(8,128)(2,1)}, u32[]{:S(2)}) copy-start(bf16[1,256,2,128]{1,3,2,0:T(8,128)(2,1)} %fusion.46) | copy-start | bytes 393220
  98.5 4.9 %copy-start.26 = (bf16[1,256,2,128]{1,3,2,0:T(8,128)(2,1)S(1)}, bf16[1,256,2,128]{1,3,2,0:T(8,128)(2,1)}, u32[]{:S(2)}) copy-start(bf16[1,256,2,128]{1,3,2,0:T(8,128)(2,1)} %fusion.45) | copy-start | bytes 393220
  100.2 7.2 %collective-permute-start.13 = (bf16[1,256,2,128]{1,3,2,0:T(8,128)(2,1)S(1)}, bf16[1,256,2,128]{1,3,2,0:T(8,128)(2,1)S(1)}, u32[]{:S(2)}, u32[]{:S(2)}) collective-permute-start(bf16[1,256,2,128]{1,3,2,0:T(8,128)(2,1)S(1)} %fusion.47), channel_id=1, source_target_pairs={{8,0},{10,2},{12,4},{14,6},{16,8},{18,10},{20,12},{22,14},{24,16},... | collective-permute-start | bytes 393224 | tf_op jit(solution)/shard_map/ppermute | solution.py:14
  102.1 9.2 %collective-permute-start.14 = (bf16[1,256,2,128]{1,3,2,0:T(8,128)(2,1)S(1)}, bf16[1,256,2,128]{1,3,2,0:T(8,128)(2,1)S(1)}, u32[]{:S(2)}, u32[]{:S(2)}) collective-permute-start(bf16[1,256,2,128]{1,3,2,0:T(8,128)(2,1)S(1)} %copy-done.27), channel_id=1, source_target_pairs={{16,0},{18,2},{20,4},{22,6},{24,8},{26,10},{28,12},{30,14},{17,1},... | collective-permute-start | bytes 393224 | tf_op jit(solution)/shard_map/ppermute | solution.py:14
  103.5 12.1 %collective-permute-start.15 = (bf16[1,256,2,128]{1,3,2,0:T(8,128)(2,1)S(1)}, bf16[1,256,2,128]{1,3,2,0:T(8,128)(2,1)S(1)}, u32[]{:S(2)}, u32[]{:S(2)}) collective-permute-start(bf16[1,256,2,128]{1,3,2,0:T(8,128)(2,1)S(1)} %copy-done.26), channel_id=1, source_target_pairs={{2,0},{4,2},{6,4},{8,6},{10,8},{12,10},{14,12},{16,14},{18,16},{20... | collective-permute-start | bytes 393224 | tf_op jit(solution)/shard_map/ppermute | solution.py:14
where the time goes:
time: 119 us; the launch traced here: 117 us
  starting transfers between devices  42 us (35%)
  matrix products  23.6 us (20%)
  waiting for transfers between devices  17.9 us (15%)
  local copies, waits for them, and re-layouts  15.6 us (13%)
  other arithmetic  9.19 us (8%)
  blocking collectives  4.66 us (4%)
  between operations  3.9 us (3%)
    ppermute x16, starting transfers between devices, passed_along(): lax.ppermute(value, axis, [(source, source + steps) for source in range(l...  42 us
    ppermute x16, waiting for transfers between devices, passed_along(): lax.ppermute(value, axis, [(source, source + steps) for source in range(l...  17.9 us
    unnamed x69, local copies, waits for them, and re-layouts  8.6 us
    dot_general x5, matrix products, per_device(): jnp.einsum('bhgus,buhgd->bshd', probabilities, grad_grouped, preferred_el...  6.28 us
    dot_general x5, matrix products, per_device(): jnp.einsum('bhgus,bshd->buhgd', probabilities, entry[1], preferred_elemen...  5.09 us
    psum x1, blocking collectives, per_device(): square_total = lax.psum(jnp.sum(attn_wide * attn_wide, axis=(2, 3)), 'head')  4.66 us
    reduce_sum x1, other arithmetic, per_device(): jnp.sum(attention_gradient.astype(jnp.float32) * attn_wide, axis=-1)  4.04 us
    dot_general x5, matrix products, per_device(): jnp.einsum('buhgd,bshd->bhgus', grad_grouped, value_block, preferred_elem...  4.03 us
  transfers between devices with their start and end apart: 16, of which 6 were waited for; matrix products, arithmetic and copies ran while one was open for 13% of the time, Pallas kernels for 0%

commit v1 on v0

v1 whole, which is shorter than its diff:
```python
import math

import jax
import jax.numpy as jnp
from jax import lax
from jax.experimental import pallas as pl
from jax.experimental.pallas import tpu as pltpu
from jax.sharding import PartitionSpec as P

epsilon = 1e-06
MESH = pl.DeviceIdType.MESH
F32 = jnp.float32
BF16 = jnp.bfloat16


def dot_nn(a, b):
    return lax.dot_general(a, b, (((1,), (0,)), ((), ())), preferred_element_type=F32)


def dot_nt(a, b):
    return lax.dot_general(a, b, (((1,), (1,)), ((), ())), preferred_element_type=F32)


def make_kernel(n, heads, levels, group, kv_heads, rows, size):
    local_heads = group * kv_heads
    scale = 1.0 / math.sqrt(size)
    c = scale * math.log2(math.e)
    features = float(local_heads * heads * size)
    slots = levels + 1
    neg, pos = -float("inf"), float("inf")

    def distance(i):
        return 2**i

    def step(i):
        return 2**i if i <= 2 else 2 ** (i - 1)

    steps = sorted({step(i) for i in range(slots)})

    def kernel(
        reach_ref, partner_ref, kv_ref, q_ref, og_ref, gain_ref,
        normed_ref, dq_ref, dk_ref, dv_ref,
        kvr, gsend, grecv, gown, wide, q_scr, sg, probs, m_scr, l_scr, mblk, acc, attn, da, delta,
        stat_own, stat_in,
        fsend, frecv, bsend, brecv, ssend, srecv,
    ):
        me = lax.axis_index("seq")
        hd = lax.axis_index("head")

        barrier = pltpu.get_barrier_semaphore()
        count = jnp.int32(heads - 1)
        for d in steps:
            @pl.when(me + d < n)
            def _():
                pl.semaphore_signal(barrier, inc=1, device_id=(me + d, hd), device_id_type=MESH)

            @pl.when(me >= d)
            def _():
                pl.semaphore_signal(barrier, inc=1, device_id=(me - d, hd), device_id_type=MESH)

            count = count + jnp.where(me + d < n, 1, 0) + jnp.where(me >= d, 1, 0)
        for o in range(1, heads):
            pl.semaphore_signal(
                barrier, inc=1, device_id=(me, lax.rem(hd + o, heads)), device_id_type=MESH
            )
        pl.semaphore_wait(barrier, count)

        def forward_copy(i, g):
            source = kv_ref.at[g] if i <= 2 else kvr.at[i - 1, g]
            return pltpu.make_async_remote_copy(
                src_ref=source, dst_ref=kvr.at[i, g],
                send_sem=fsend.at[i, g], recv_sem=frecv.at[i, g],
                device_id=(me + step(i), hd), device_id_type=MESH,
            )

        def backward_copy(i, g):
            return pltpu.make_async_remote_copy(
                src_ref=gsend.at[i, g], dst_ref=grecv.at[i, g],
                send_sem=bsend.at[i, g], recv_sem=brecv.at[i, g],
                device_id=(me - step(i), hd), device_id_type=MESH,
            )

        def sends(i):
            if i <= 2:
                return me + step(i) < n
            return (me + step(i) < n) & (me >= step(i))

        def has(i):
            return me >= distance(i)

        def gets_back(i):
            return (me + step(i) < n) & (me + step(i) >= distance(i))

        for i in [i for i in (2, 0, 1) if i < slots]:
            @pl.when(sends(i))
            def _():
                for g in range(kv_heads):
                    forward_copy(i, g).start()

        wide[...] = q_ref[...].astype(F32).reshape(rows * local_heads, size)
        for h in range(local_heads):
            q_scr[h] = wide[pl.ds(h, rows, stride=local_heads), :].astype(BF16)

        key_pos = lax.broadcasted_iota(jnp.int32, (rows, rows), 0)
        query_pos = lax.broadcasted_iota(jnp.int32, (rows, rows), 1)

        def forward_block(pi, g, kv):
            key, value = kv[0], kv[1]
            value_t = value.T
            for k in range(group):
                h = g * group + k
                s = dot_nt(key, q_scr[h])
                if pi == 0:
                    s = jnp.where(key_pos <= query_pos, s, neg)
                elif pi == 1:
                    s = jnp.where(key_pos >= rows - reach_ref[0, 0], s, neg)
                top = jnp.max(s, axis=0, keepdims=True)
                if pi >= 2:
                    on = partner_ref[0, pi - 2] == 1
                    top = top + jnp.where(on, 0.0, neg)
                if pi == 0:
                    m = top
                else:
                    old = m_scr[h]
                    m = jnp.maximum(old, top)
                shift = m * c
                if pi >= 2:
                    shift = shift + jnp.where(on, 0.0, pos)
                p = jnp.exp2(s * c - shift)
                total = jnp.sum(p, axis=0, keepdims=True)
                pb = p.astype(BF16)
                probs[pi, h] = pb
                part = dot_nn(value_t, pb)
                if pi == 0:
                    l_scr[h] = total
                    acc[h] = part
                else:
                    alpha = jnp.exp2((old - m) * c)
                    l_scr[h] = l_scr[h] * alpha + total
                    acc[h] = acc[h] * alpha + part
                m_scr[h] = m
                mblk[pi, h] = m

        @pl.loop(0, kv_heads)
        def _(g):
            forward_block(0, g, kv_ref.at[g])

        wide[...] = og_ref[...].astype(F32).reshape(rows * local_heads, size)
        for h in range(local_heads):
            piece = wide[pl.ds(h, rows, stride=local_heads), :] * gain_ref[h : h + 1, :]
            sg[h] = piece.T

        for i in range(slots):
            @pl.when(has(i))
            def _():
                @pl.loop(0, kv_heads)
                def _(g):
                    forward_copy(i, g).wait_recv()
                    if i >= 2 and i + 1 < slots:
                        @pl.when(sends(i + 1))
                        def _():
                            forward_copy(i + 1, g).start()
                    forward_block(i + 1, g, kvr.at[i, g])

        def first_sums(h, carry):
            square, dot = carry
            a = (acc[h] * (1.0 / l_scr[h])).astype(BF16)
            attn[h] = a
            af = a.astype(F32)
            return (
                square + jnp.sum(af * af, axis=0, keepdims=True),
                dot + jnp.sum(sg[h] * af, axis=0, keepdims=True),
            )

        zero = jnp.zeros((1, rows), F32)
        square, dot = lax.fori_loop(0, local_heads, first_sums, (zero, zero))
        stat_own[...] = jnp.zeros((8, rows), F32)
        stat_own[0:1, :] = square
        stat_own[1:2, :] = dot

        def stat_copy(o):
            return pltpu.make_async_remote_copy(
                src_ref=stat_own, dst_ref=stat_in.at[o - 1],
                send_sem=ssend.at[o - 1], recv_sem=srecv.at[o - 1],
                device_id=(me, lax.rem(hd + o, heads)), device_id_type=MESH,
            )

        for o in range(1, heads):
            stat_copy(o).start()
        for o in range(1, heads):
            stat_copy(o).wait()
            square = square + stat_in[o - 1, 0:1, :]
            dot = dot + stat_in[o - 1, 1:2, :]
        inverse = lax.rsqrt(square / features + epsilon)
        pull = dot * (inverse * inverse * inverse) / features

        @pl.loop(0, local_heads)
        def _(h):
            af = attn[h].astype(F32)
            grad = (sg[h] * inverse - af * pull).astype(BF16)
            da[h] = grad
            delta[h] = jnp.sum(grad.astype(F32) * af, axis=0, keepdims=True)
            acc[h] = jnp.zeros((size, rows), F32)

        def backward_block(pi, g, kv):
            key, value = kv[0], kv[1]
            key_t = key.T
            dk = jnp.zeros((rows, size), F32)
            dv = jnp.zeros((rows, size), F32)
            for k in range(group):
                h = g * group + k
                r = jnp.exp2((mblk[pi, h] - m_scr[h]) * c) / l_scr[h]
                dar = (da[h].astype(F32) * r).astype(BF16)
                dp = dot_nn(value, dar)
                pb = probs[pi, h]
                ds = (pb.astype(F32) * (dp - delta[h] * r)).astype(BF16)
                acc[h] += dot_nn(key_t, ds)
                dk = dk + dot_nn(ds, q_scr[h])
                dv = dv + dot_nt(pb, dar)
            return dk, dv

        for i in [*range(slots - 1, 1, -1), *range(min(slots, 2) - 1, -1, -1)]:
            @pl.when(has(i))
            def _():
                @pl.loop(0, kv_heads)
                def _(g):
                    dk, dv = backward_block(i + 1, g, kvr.at[i, g])
                    gown[g, 0] = dk
                    gown[g, 1] = dv
                    if i >= 2 and i + 1 < slots:
                        @pl.when(gets_back(i + 1))
                        def _():
                            backward_copy(i + 1, g).wait_recv()
                            gown[g] += grecv[i + 1, g].astype(F32)
                    gsend[i, g] = gown[g].astype(BF16)
                    backward_copy(i, g).start()

        @pl.loop(0, kv_heads)
        def _(g):
            dk, dv = backward_block(0, g, kv_ref.at[g])
            gown[g, 0] = dk
            gown[g, 1] = dv

        for h in range(local_heads):
            dq_ref[:, h * size : (h + 1) * size] = (acc[h] * scale).T.astype(BF16)
            tile = (attn[h].astype(F32) * inverse).T * gain_ref[h : h + 1, :]
            normed_ref[:, h * size : (h + 1) * size] = tile.astype(BF16)

        for i in [i for i in (0, 1, 2) if i < slots]:
            @pl.when(gets_back(i))
            def _():
                for g in range(kv_heads):
                    backward_copy(i, g).wait_recv()
                    gown[g] += grecv[i, g].astype(F32)
        for g in range(kv_heads):
            dk_ref[:, g * size : (g + 1) * size] = (gown[g, 0] * scale).astype(BF16)
            dv_ref[:, g * size : (g + 1) * size] = gown[g, 1].astype(BF16)

        for i in range(slots):
            @pl.when(sends(i))
            def _():
                for g in range(kv_heads):
                    forward_copy(i, g).wait_send()

            @pl.when(has(i))
            def _():
                for g in range(kv_heads):
                    backward_copy(i, g).wait_send()

    return kernel


def solution(mesh):
    n, heads = mesh.shape["seq"], mesh.shape["head"]
    levels = len([j for j in range(1, 11) if 2 ** (j + 1) <= n])

    def per_device(queries, keys, values, norm_gain, out_grad, window_reach, partner_mask):
        _, rows, local_heads, size = queries.shape
        kv_heads = keys.shape[2]
        group = local_heads // kv_heads
        slots = levels + 1
        k2 = keys[0].transpose(1, 0, 2)
        v2 = values[0].transpose(1, 0, 2)
        kv = jnp.stack([k2, v2], axis=1)
        vmem = pl.BlockSpec(memory_space=pltpu.VMEM)
        smem = pl.BlockSpec(memory_space=pltpu.SMEM)
        dma = pltpu.SemaphoreType.DMA
        wide_shape = (rows, local_heads * size)
        thin_shape = (rows, kv_heads * size)
        normed, dq, dk, dv = pl.pallas_call(
            make_kernel(n, heads, levels, group, kv_heads, rows, size),
            out_shape=[
                jax.ShapeDtypeStruct(wide_shape, BF16),
                jax.ShapeDtypeStruct(wide_shape, BF16),
                jax.ShapeDtypeStruct(thin_shape, BF16),
                jax.ShapeDtypeStruct(thin_shape, BF16),
            ],
            in_specs=[smem, smem, vmem, vmem, vmem, vmem],
            out_specs=[vmem] * 4,
            scratch_shapes=[
                pltpu.VMEM((slots, kv_heads, 2, rows, size), BF16),
                pltpu.VMEM((slots, kv_heads, 2, rows, size), BF16),
                pltpu.VMEM((slots, kv_heads, 2, rows, size), BF16),
                pltpu.VMEM((kv_heads, 2, rows, size), F32),
                pltpu.VMEM((rows * local_heads, size), F32),
                pltpu.VMEM((local_heads, rows, size), BF16),
                pltpu.VMEM((local_heads, size, rows), F32),
                pltpu.VMEM((slots + 1, local_heads, rows, rows), BF16),
                pltpu.VMEM((local_heads, 1, rows), F32),
                pltpu.VMEM((local_heads, 1, rows), F32),
                pltpu.VMEM((slots + 1, local_heads, 1, rows), F32),
                pltpu.VMEM((local_heads, size, rows), F32),
                pltpu.VMEM((local_heads, size, rows), BF16),
                pltpu.VMEM((local_heads, size, rows), BF16),
                pltpu.VMEM((local_heads, 1, rows), F32),
                pltpu.VMEM((8, rows), F32),
                pltpu.VMEM((max(heads - 1, 1), 8, rows), F32),
                dma((slots, kv_heads)), dma((slots, kv_heads)),
                dma((slots, kv_heads)), dma((slots, kv_heads)),
                dma((max(heads - 1, 1),)), dma((max(heads - 1, 1),)),
            ],
            compiler_params=pltpu.CompilerParams(
                collective_id=0, has_side_effects=True, vmem_limit_bytes=48 * 1024 * 1024
            ),
        )(
            window_reach, partner_mask[0], kv, queries[0], out_grad[0], norm_gain
        )
        full = (1, rows, local_heads, size)
        thin = (1, rows, kv_heads, size)
        return normed.reshape(full), dq.reshape(full), dk.reshape(thin), dv.reshape(thin)

    wide_spec = P(None, "seq", "head", None)
    return jax.shard_map(
        per_device,
        mesh=mesh,
        in_specs=(
            wide_spec, wide_spec, wide_spec, P("head", None), wide_spec,
            P(None, "seq"), P(None, "seq", None),
        ),
        out_specs=(wide_spec,) * 4,
        check_vma=False,
    )
```

time: 119 us -> 61.7 us (0.52); the launches traced: 117 us -> 61.6 us
  Pallas kernels: 0 us -> 54.6 us
  starting transfers between devices: 42 us -> 0 us
  matrix products: 23.6 us -> 0 us
  waiting for transfers between devices: 17.9 us -> 0 us
  local copies, waits for them, and re-layouts: 15.6 us -> 5.61 us
  other arithmetic: 9.19 us -> 0.03 us
  blocking collectives: 4.66 us -> 0 us
  between operations: 3.9 us -> 1.33 us
    pallas_call x0 -> x1, Pallas kernels: none -> 54.6 us  [per_device(): pl.pallas_call(make_kernel(n, heads, levels, group, kv_heads, rows, size)...]
    ppermute x16 -> x0, starting transfers between devices: 42 us -> none  [passed_along(): lax.ppermute(value, axis, [(source, source + steps) for source in range(l...]
    dot_general x30 -> x0, matrix products: 23.6 us -> none  [the longest x5 6.28 us: per_device(): jnp.einsum('bhgus,buhgd->bshd', probabilities, grad_grouped, preferred_el...]
    ppermute x16 -> x0, waiting for transfers between devices: 17.9 us -> none  [passed_along(): lax.ppermute(value, axis, [(source, source + steps) for source in range(l...]
    reduce_sum x5 -> x0, other arithmetic: 8.4 us -> none  [the longest x1 4.04 us: per_device(): jnp.sum(attention_gradient.astype(jnp.float32) * attn_wide, axis=-1)]
    unnamed x69 -> x10, local copies, waits for them, and re-layouts: 8.6 us -> 3.14 us
    psum x1 -> x0, blocking collectives: 4.66 us -> none  [per_device(): square_total = lax.psum(jnp.sum(attn_wide * attn_wide, axis=(2, 3)), 'head')]
    convert_element_type x1 -> x0, local copies, waits for them, and re-layouts: 2.61 us -> none  [per_device(): attn_wide = attention.astype(jnp.float32)]
  transfers between devices with their start and end apart: 16 -> 0, of which waited for: 6 -> 0; matrix products, arithmetic and copies ran while one was open for 13% -> 0% of each run, Pallas kernels for 0% -> 0%
where the time goes in v1:
time: 61.7 us; the launch traced here: 61.6 us
  Pallas kernels  54.6 us (88%)
  local copies, waits for them, and re-layouts  5.61 us (9%)
  between operations  1.33 us (2%)
    pallas_call x1, Pallas kernels, per_device(): pl.pallas_call(make_kernel(n, heads, levels, group, kv_heads, rows, size)...  54.6 us
    unnamed x10, local copies, waits for them, and re-layouts  3.14 us

profile of v1, /device:TPU:11, one launch (start us, length us, event | category | flops | bytes accessed | tf_op | source)
XLA Modules:
  0.0 61.6 jit_solution(16310191044456416486)
XLA Ops:
  1.3 0.0 copy-start
  1.3 0.0 copy-start.1
  1.3 1.1 %copy_bitcast_fusion = (bf16[2,1,256,128]{3,2,1,0:T(8,128)(2,1)S(1)}, bf16[2,1,256,128]{3,2,1,0:T(8,128)(2,1)S(1)}) fusion(bf16[1,256,2,128]{3,2,1,0:T(2,128)(2,1)} %param.9, bf16[1,256,2,128]{3,2,1,0:T(2,128)(2,1)} %param.8), kind=kLoop, calls=%fused_computation.1 | loop fusion | bytes 524288 | tf_op jit(solution)/shard_map/stack | solution.py:284
  2.4 0.0 copy-start.3
  2.4 0.0 copy-done
  2.4 0.2 copy-done.1
  2.6 0.5 copy-done.3
  3.1 0.0 copy-start.2
  3.1 0.7 %copy-done.2 = f32[8,128]{1,0:T(8,128)S(1)} copy-done((f32[8,128]{1,0:T(8,128)S(1)}, f32[8,128]{1,0:T(8,128)}, u32[]{:S(2)}) %copy-start.2) | copy-done | bytes 4120
  3.8 54.6 %shard_map.102 = (bf16[256,1024]{1,0:T(8,128)(2,1)S(1)}, bf16[256,1024]{1,0:T(8,128)(2,1)S(1)}, bf16[256,256]{1,0:T(8,128)(2,1)S(1)}, bf16[256,256]{1,0:T(8,128)(2,1)S(1)}) custom-call(s32[1,1]{1,0:T(1,128)S(6)} %copy.17.reach_ref, s32[1,3]{1,0:T(1,128)S(1)} %bitcast.25, bf16[2,2,256,128]{3,2,1,0:T(8,128)(2,1)S(1)} %pad_maximum_fusion.kv_ref, ...), custom_call_target="tpu_custom_call" | custom-call | tf_op jit(solution)/shard_map/pallas_call | solution.py:290
  58.4 0.9 %copy.13 = bf16[32,8,8,128]{3,2,1,0:T(8,128)(2,1)} copy(bf16[32,8,8,128]{3,1,2,0:T(8,128)(2,1)S(1)} %bitcast.24) | data formatting | bytes 1048576
  59.3 0.9 %copy.14 = bf16[32,8,8,128]{3,2,1,0:T(8,128)(2,1)} copy(bf16[32,8,8,128]{3,1,2,0:T(8,128)(2,1)S(1)} %bitcast.23) | data formatting | bytes 1048576
  60.2 0.7 %reshape.22 = bf16[1,256,2,128]{3,2,1,0:T(2,128)(2,1)} reshape(bf16[256,256]{1,0:T(8,128)(2,1)S(1)} %get-tuple-element.10) | data formatting | bytes 262144 | tf_op jit(solution)/shard_map/reshape | solution.py:330
  60.9 0.7 %reshape.23 = bf16[1,256,2,128]{3,2,1,0:T(2,128)(2,1)} reshape(bf16[256,256]{1,0:T(8,128)(2,1)S(1)} %get-tuple-element.11) | data formatting | bytes 262144 | tf_op jit(solution)/shard_map/reshape | solution.py:330
  (1 shorter events, 0.0 us)
Async XLA Ops:
  1.3 1.2 %copy-start = (bf16[1,256,8,128]{3,2,1,0:T(8,128)(2,1)S(1)}, bf16[1,256,8,128]{3,2,1,0:T(8,128)(2,1)}, u32[]{:S(2)}) copy-start(bf16[1,256,8,128]{3,2,1,0:T(8,128)(2,1)} %param.7) | copy-start | bytes 1572868
  1.3 1.3 %copy-start.1 = (bf16[1,256,8,128]{3,2,1,0:T(8,128)(2,1)S(1)}, bf16[1,256,8,128]{3,2,1,0:T(8,128)(2,1)}, u32[]{:S(2)}) copy-start(bf16[1,256,8,128]{3,2,1,0:T(8,128)(2,1)} %param.11) | copy-start | bytes 1572868
  2.4 0.7 %copy-start.3 = (s32[1,1,3]{2,1,0:T(1,128)S(1)}, s32[1,1,3]{2,1,0:T(1,128)}, u32[]{:S(2)}) copy-start(s32[1,1,3]{2,1,0:T(1,128)} %param.13) | copy-start | bytes 40
  3.1 0.7 %copy-start.2 = (f32[8,128]{1,0:T(8,128)S(1)}, f32[8,128]{1,0:T(8,128)}, u32[]{:S(2)}) copy-start(f32[8,128]{1,0:T(8,128)} %gain_ref.1) | copy-start | bytes 12292

commit v2 on v1

--- a/solution.py
+++ b/solution.py
@@ -65,37 +65,59 @@
             )
         pl.semaphore_wait(barrier, count)
 
-        def forward_copy(i, g):
-            source = kv_ref.at[g] if i <= 2 else kvr.at[i - 1, g]
+        even = lax.rem(me, 2) == 0
+        low = lax.rem(me, 4) < 2
+
+        def has(i):
+            return me >= distance(i)
+
+        def gets_back(i):
+            return (me + step(i) < n) & (me >= step(i))
+
+        routes = {
+            "own2": (me + 4 < n, None, 2, me + 4),
+            "own1": (low, None, 1, me + 2),
+            "own0": (even, None, 0, me + 1),
+            "pass1": (jnp.logical_not(low) & has(2), 2, 1, me - 2),
+            "pass0": (jnp.logical_not(even) & has(1), 1, 0, me - 1),
+        }
+        for i in range(3, slots):
+            routes[i] = ((me + step(i) < n) & has(i - 1), i - 1, i, me + step(i))
+        order = {name: at for at, name in enumerate(routes)}
+
+        def route_copy(name, g):
+            _, source, slot, target = routes[name]
             return pltpu.make_async_remote_copy(
-                src_ref=source, dst_ref=kvr.at[i, g],
-                send_sem=fsend.at[i, g], recv_sem=frecv.at[i, g],
-                device_id=(me + step(i), hd), device_id_type=MESH,
-            )
+                src_ref=kv_ref.at[g] if source is None else kvr.at[source, g],
+                dst_ref=kvr.at[slot, g],
+                send_sem=fsend.at[order[name], g], recv_sem=frecv.at[slot, g],
+                device_id=(target, hd), device_id_type=MESH,
+            )
+
+        def send(name, g):
+            @pl.when(routes[name][0])
+            def _():
+                route_copy(name, g).start()
+
+        def arrived(i, g):
+            route_copy({0: "own0", 1: "own1", 2: "own2"}.get(i, i), g).wait_recv()
 
         def backward_copy(i, g):
+            if i == 0:
+                target = jnp.where(even, me + 1, me - 1)
+            elif i == 1:
+                target = jnp.where(low, me + 2, me - 2)
+            else:
+                target = me - step(i)
             return pltpu.make_async_remote_copy(
                 src_ref=gsend.at[i, g], dst_ref=grecv.at[i, g],
                 send_sem=bsend.at[i, g], recv_sem=brecv.at[i, g],
-                device_id=(me - step(i), hd), device_id_type=MESH,
-            )
-
-        def sends(i):
-            if i <= 2:
-                return me + step(i) < n
-            return (me + step(i) < n) & (me >= step(i))
-
-        def has(i):
-            return me >= distance(i)
-
-        def gets_back(i):
-            return (me + step(i) < n) & (me + step(i) >= distance(i))
-
-        for i in [i for i in (2, 0, 1) if i < slots]:
-            @pl.when(sends(i))
-            def _():
-                for g in range(kv_heads):
-                    forward_copy(i, g).start()
+                device_id=(target, hd), device_id_type=MESH,
+            )
+
+        for name in ("own2", "own1", "own0"):
+            for g in range(kv_heads):
+                send(name, g)
 
         wide[...] = q_ref[...].astype(F32).reshape(rows * local_heads, size)
         for h in range(local_heads):
@@ -145,21 +167,32 @@
         def _(g):
             forward_block(0, g, kv_ref.at[g])
 
+            @pl.when(has(2))
+            def _():
+                arrived(2, g)
+                if slots > 3:
+                    send(3, g)
+                send("pass1", g)
+
         wide[...] = og_ref[...].astype(F32).reshape(rows * local_heads, size)
         for h in range(local_heads):
             piece = wide[pl.ds(h, rows, stride=local_heads), :] * gain_ref[h : h + 1, :]
             sg[h] = piece.T
 
-        for i in range(slots):
+        for i in (2, 1, 0, *range(3, slots)):
             @pl.when(has(i))
             def _():
+                if i == 1:
+                    for g in range(kv_heads):
+                        arrived(1, g)
+                        send("pass0", g)
+
                 @pl.loop(0, kv_heads)
                 def _(g):
-                    forward_copy(i, g).wait_recv()
-                    if i >= 2 and i + 1 < slots:
-                        @pl.when(sends(i + 1))
-                        def _():
-                            forward_copy(i + 1, g).start()
+                    if i == 0 or i >= 3:
+                        arrived(i, g)
+                    if i >= 3 and i + 1 < slots:
+                        send(i + 1, g)
                     forward_block(i + 1, g, kvr.at[i, g])
 
         def first_sums(h, carry):
@@ -219,7 +252,15 @@
                 dv = dv + dot_nt(pb, dar)
             return dk, dv
 
-        for i in [*range(slots - 1, 1, -1), *range(min(slots, 2) - 1, -1, -1)]:
+        for i in (*range(slots - 1, 2, -1), 0, 1, 2):
+            feeds = []
+            if i == 1:
+                feeds.append((0, jnp.logical_not(even)))
+            if i == 2:
+                feeds.append((1, jnp.logical_not(low) & (me >= 6)))
+            if i >= 2 and i + 1 < slots:
+                feeds.append((i + 1, gets_back(i + 1)))
+
             @pl.when(has(i))
             def _():
                 @pl.loop(0, kv_heads)
@@ -227,11 +268,11 @@
                     dk, dv = backward_block(i + 1, g, kvr.at[i, g])
                     gown[g, 0] = dk
                     gown[g, 1] = dv
-                    if i >= 2 and i + 1 < slots:
-                        @pl.when(gets_back(i + 1))
+                    for feed, cond in feeds:
+                        @pl.when(cond)
                         def _():
-                            backward_copy(i + 1, g).wait_recv()
-                            gown[g] += grecv[i + 1, g].astype(F32)
+                            backward_copy(feed, g).wait_recv()
+                            gown[g] += grecv[feed, g].astype(F32)
                     gsend[i, g] = gown[g].astype(BF16)
                     backward_copy(i, g).start()
 
@@ -246,8 +287,8 @@
             tile = (attn[h].astype(F32) * inverse).T * gain_ref[h : h + 1, :]
             normed_ref[:, h * size : (h + 1) * size] = tile.astype(BF16)
 
-        for i in [i for i in (0, 1, 2) if i < slots]:
-            @pl.when(gets_back(i))
+        for i, cond in ((0, even), (1, low), (2, me + 4 < n)):
+            @pl.when(cond)
             def _():
                 for g in range(kv_heads):
                     backward_copy(i, g).wait_recv()
@@ -256,12 +297,13 @@
             dk_ref[:, g * size : (g + 1) * size] = (gown[g, 0] * scale).astype(BF16)
             dv_ref[:, g * size : (g + 1) * size] = gown[g, 1].astype(BF16)
 
+        for name in routes:
+            @pl.when(routes[name][0])
+            def _():
+                for g in range(kv_heads):
+                    route_copy(name, g).wait_send()
+
         for i in range(slots):
-            @pl.when(sends(i))
-            def _():
-                for g in range(kv_heads):
-                    forward_copy(i, g).wait_send()
-
             @pl.when(has(i))
             def _():
                 for g in range(kv_heads):
@@ -315,7 +357,7 @@
                 pltpu.VMEM((local_heads, 1, rows), F32),
                 pltpu.VMEM((8, rows), F32),
                 pltpu.VMEM((max(heads - 1, 1), 8, rows), F32),
-                dma((slots, kv_heads)), dma((slots, kv_heads)),
+                dma((slots + 2, kv_heads)), dma((slots, kv_heads)),
                 dma((slots, kv_heads)), dma((slots, kv_heads)),
                 dma((max(heads - 1, 1),)), dma((max(heads - 1, 1),)),
             ],

time: 61.7 us -> 50.2 us (0.81)
  the two profiles are of different devices: /device:TPU:11 before, /device:TPU:10 now
where the time goes in v2:
time: 50.2 us; the launch traced here: 50 us
  Pallas kernels  43 us (86%)
  local copies, waits for them, and re-layouts  5.61 us (11%)
  between operations  1.33 us (3%)
    pallas_call x1, Pallas kernels, per_device(): pl.pallas_call(make_kernel(n, heads, levels, group, kv_heads, rows, size)...  43 us
    unnamed x10, local copies, waits for them, and re-layouts  3.14 us
    another operation x1, local copies, waits for them, and re-layouts, per_device(): kv = jnp.stack([k2, v2], axis=1)  1.09 us

profile of v2, /device:TPU:10, one launch (start us, length us, event | category | flops | bytes accessed | tf_op | source)
XLA Modules:
  0.0 50.0 jit_solution(10949757670609754012)
XLA Ops:
  1.3 0.0 copy-start
  1.3 0.0 copy-start.1
  1.3 1.1 %copy_bitcast_fusion = (bf16[2,1,256,128]{3,2,1,0:T(8,128)(2,1)S(1)}, bf16[2,1,256,128]{3,2,1,0:T(8,128)(2,1)S(1)}) fusion(bf16[1,256,2,128]{3,2,1,0:T(2,128)(2,1)} %param.9, bf16[1,256,2,128]{3,2,1,0:T(2,128)(2,1)} %param.8), kind=kLoop, calls=%fused_computation.1 | loop fusion | bytes 524288 | tf_op jit(solution)/shard_map/stack | solution.py:326
  2.4 0.0 copy-start.3
  2.4 0.0 copy-done
  2.4 0.2 copy-done.1
  2.6 0.5 copy-done.3
  3.1 0.0 copy-start.2
  3.1 0.7 %copy-done.2 = f32[8,128]{1,0:T(8,128)S(1)} copy-done((f32[8,128]{1,0:T(8,128)S(1)}, f32[8,128]{1,0:T(8,128)}, u32[]{:S(2)}) %copy-start.2) | copy-done | bytes 4120
  3.8 43.0 %shard_map.102 = (bf16[256,1024]{1,0:T(8,128)(2,1)S(1)}, bf16[256,1024]{1,0:T(8,128)(2,1)S(1)}, bf16[256,256]{1,0:T(8,128)(2,1)S(1)}, bf16[256,256]{1,0:T(8,128)(2,1)S(1)}) custom-call(s32[1,1]{1,0:T(1,128)S(6)} %copy.17.reach_ref, s32[1,3]{1,0:T(1,128)S(1)} %bitcast.25, bf16[2,2,256,128]{3,2,1,0:T(8,128)(2,1)S(1)} %pad_maximum_fusion.kv_ref, ...), custom_call_target="tpu_custom_call" | custom-call | tf_op jit(solution)/shard_map/pallas_call | solution.py:332
  46.8 0.9 %copy.13 = bf16[32,8,8,128]{3,2,1,0:T(8,128)(2,1)} copy(bf16[32,8,8,128]{3,1,2,0:T(8,128)(2,1)S(1)} %bitcast.24) | data formatting | bytes 1048576
  47.7 0.9 %copy.14 = bf16[32,8,8,128]{3,2,1,0:T(8,128)(2,1)} copy(bf16[32,8,8,128]{3,1,2,0:T(8,128)(2,1)S(1)} %bitcast.23) | data formatting | bytes 1048576
  48.6 0.7 %reshape.22 = bf16[1,256,2,128]{3,2,1,0:T(2,128)(2,1)} reshape(bf16[256,256]{1,0:T(8,128)(2,1)S(1)} %get-tuple-element.10) | data formatting | bytes 262144 | tf_op jit(solution)/shard_map/reshape | solution.py:372
  49.3 0.7 %reshape.23 = bf16[1,256,2,128]{3,2,1,0:T(2,128)(2,1)} reshape(bf16[256,256]{1,0:T(8,128)(2,1)S(1)} %get-tuple-element.11) | data formatting | bytes 262144 | tf_op jit(solution)/shard_map/reshape | solution.py:372
  (1 shorter events, 0.0 us)
Async XLA Ops:
  1.3 1.2 %copy-start = (bf16[1,256,8,128]{3,2,1,0:T(8,128)(2,1)S(1)}, bf16[1,256,8,128]{3,2,1,0:T(8,128)(2,1)}, u32[]{:S(2)}) copy-start(bf16[1,256,8,128]{3,2,1,0:T(8,128)(2,1)} %param.7) | copy-start | bytes 1572868
  1.3 1.3 %copy-start.1 = (bf16[1,256,8,128]{3,2,1,0:T(8,128)(2,1)S(1)}, bf16[1,256,8,128]{3,2,1,0:T(8,128)(2,1)}, u32[]{:S(2)}) copy-start(bf16[1,256,8,128]{3,2,1,0:T(8,128)(2,1)} %param.11) | copy-start | bytes 1572868
  2.4 0.7 %copy-start.3 = (s32[1,1,3]{2,1,0:T(1,128)S(1)}, s32[1,1,3]{2,1,0:T(1,128)}, u32[]{:S(2)}) copy-start(s32[1,1,3]{2,1,0:T(1,128)} %param.13) | copy-start | bytes 40
  3.1 0.7 %copy-start.2 = (f32[8,128]{1,0:T(8,128)S(1)}, f32[8,128]{1,0:T(8,128)}, u32[]{:S(2)}) copy-start(f32[8,128]{1,0:T(8,128)} %gain_ref.1) | copy-start | bytes 12292
